TPU v7x, 32 devices: a whole 2x2x4 slice. The times are simulated.
32 devices in a mesh: blk: 8 (over y, x, core), exp: 4 (over z).
Axes of the slice: x: 2, y: 2, z: 4, core: 2. Of those that a mesh axis runs over, the one named last changes fastest.
Arguments:
- residual_deposit_sequence: bfloat16 [4, 1024, 1536], P('exp', 'blk'), may hold values from -60 to 60
- premix_rescaler: float32 [1536], replicated, may hold values from 0.25 to 1.75
- asking_projector: bfloat16 [1536, 1536], P(None, 'exp'), may hold values from -0.15625 to 0.15625
- lookup_projector: bfloat16 [1536, 512], P(None, 'exp'), may hold values from -0.15625 to 0.15625
- content_projector: bfloat16 [1536, 512], P(None, 'exp'), may hold values from -0.15625 to 0.15625
- final_projector: bfloat16 [1536, 1536], P('exp'), may hold values from -0.15625 to 0.15625
- logit_multipliers: float32 [12], replicated, may hold values from 1.5 to 6
- premixture_rescaler: float32 [1536], replicated, may hold values from 0.25 to 1.75
- specialist_switch_tensor: bfloat16 [8, 1536, 384], P('exp'), may hold values from -0.15625 to 0.15625
- specialist_widen_tensor: bfloat16 [8, 1536, 384], P('exp'), may hold values from -0.15625 to 0.15625
- specialist_shrink_tensor: bfloat16 [8, 384, 1536], P('exp'), may hold values from -0.3125 to 0.3125
- picked_specialist_labels: int32 [4, 1024, 2], P(None, 'blk'), may hold values from 0 to 7, all different within a row; in each aligned block of 128 rows (0 to 127, 128 to 255, ..., all dimensions but the last counted through in order) at most 64 rows name the same one
- specialist_shares: float32 [4, 1024, 2], P(None, 'blk'), may hold values from 0.1 to 1
Outputs:
- attention_update: bfloat16 [4, 1024, 1536], P('exp', 'blk')
- expert_update: bfloat16 [4, 1024, 1536], P('exp', 'blk')
Inputs may be any that keep to these rules, and one draw needn't show every extreme that they name: `picked_specialist_labels`: the 2 ids of a hit differ. Within each event's 128 hits on one index of blk (an aligned block of 128 rows) no expert is named by more than 64 hits, a bound that some block reaches.
All inputs are finite; a program needn't handle non-finite values.
Results may differ from a plain program's by a relative error of at most 0.019.
Values may be sent and summed in bfloat16 or wider, within the bound.
A program may use at most 192 MiB of HBM per device.

v0:
```python
import math
import jax
import jax.numpy as jnp
from jax import lax
from jax.sharding import PartitionSpec as P

D = 1536
PER_LANE_DIM = 128
TOP = 2
CAP = 64


def norm_rows(values, norm_gain):
    widened = values.astype(jnp.float32)
    return (
        widened * lax.rsqrt(jnp.mean(widened * widened, axis=-1, keepdims=True) + 1e-05) * norm_gain
    )


def head_norm(values):
    return values * lax.rsqrt(jnp.mean(values * values, axis=-1, keepdims=True) + 1e-06)


def attend_hits(
    rescaled_entries,
    asking_projector,
    lookup_projector,
    content_projector,
    final_projector,
    logit_multipliers,
):
    events, row_count, model_width = rescaled_entries.shape
    common_key_heads = lookup_projector.shape[1] // PER_LANE_DIM
    local_lane_count = asking_projector.shape[1] // PER_LANE_DIM
    askers_per_lookup = local_lane_count // common_key_heads
    query_heads = jnp.einsum(
        "std,de->ste", rescaled_entries, asking_projector, preferred_element_type=jnp.float32
    )
    query_heads = head_norm(
        query_heads.reshape(events, row_count, common_key_heads, askers_per_lookup, PER_LANE_DIM)
    ).astype(jnp.bfloat16)
    key_heads = jnp.einsum(
        "std,de->ste", rescaled_entries, lookup_projector, preferred_element_type=jnp.float32
    )
    key_heads = head_norm(
        key_heads.reshape(events, row_count, common_key_heads, PER_LANE_DIM)
    ).astype(jnp.bfloat16)
    value_heads = jnp.einsum(
        "std,de->ste", rescaled_entries, content_projector, preferred_element_type=jnp.float32
    )
    value_heads = value_heads.reshape(events, row_count, common_key_heads, PER_LANE_DIM).astype(
        jnp.bfloat16
    )
    inverse_root_dim = (logit_multipliers / math.sqrt(PER_LANE_DIM)).reshape(
        common_key_heads, askers_per_lookup
    )
    key_piece = lax.all_gather(key_heads, "blk", axis=1, tiled=True)
    value_piece = lax.all_gather(value_heads, "blk", axis=1, tiled=True)
    scores = jnp.einsum(
        "sikgd,sjkd->skgij", query_heads, key_piece, preferred_element_type=jnp.float32
    )
    expo = jnp.exp(scores * inverse_root_dim[None, :, :, None, None])
    totals = jnp.sum(expo, axis=-1)
    mixture = jnp.einsum(
        "skgij,sjkd->skgid",
        expo.astype(jnp.bfloat16),
        value_piece,
        preferred_element_type=jnp.float32,
    )
    totals, mixture = (totals, mixture)
    heads_out = head_norm(mixture / totals[..., None]).astype(jnp.bfloat16)
    out_blocks = final_projector.reshape(
        common_key_heads, askers_per_lookup, PER_LANE_DIM, model_width
    )
    return jnp.einsum("skgid,kgde->sie", heads_out, out_blocks, preferred_element_type=jnp.float32)


def slot_tables(chosen, expert_count):
    events, row_count, top_count = chosen.shape
    flat_ids = chosen.reshape(events, row_count * top_count)
    onehot = (
        flat_ids[:, :, None] == jnp.arange(expert_count, dtype=jnp.int32)[None, None, :]
    ).astype(jnp.int32)
    before = jnp.cumsum(onehot, axis=1) - onehot
    slot_of = jnp.sum(before * onehot, axis=2)
    source_rows = jnp.arange(row_count * top_count, dtype=jnp.int32)[None, :] // top_count
    event_index = jnp.arange(events, dtype=jnp.int32)[:, None]
    tables = (
        jnp.zeros((events, expert_count, CAP), jnp.int32)
        .at[event_index, flat_ids, slot_of]
        .set(source_rows)
    )
    return (slot_of, tables)


def run_experts(
    batched, specialist_switch_tensor, specialist_widen_tensor, specialist_shrink_tensor
):
    gate_act = jnp.einsum(
        "sjcd,jdf->sjcf", batched, specialist_switch_tensor, preferred_element_type=jnp.float32
    )
    up_act = jnp.einsum(
        "sjcd,jdf->sjcf", batched, specialist_widen_tensor, preferred_element_type=jnp.float32
    )
    hidden = (jax.nn.silu(gate_act) * up_act).astype(jnp.bfloat16)
    return jnp.einsum(
        "sjcf,jfd->sjcd", hidden, specialist_shrink_tensor, preferred_element_type=jnp.float32
    ).astype(jnp.bfloat16)


def body(
    residual_deposit_sequence,
    premix_rescaler,
    asking_projector,
    lookup_projector,
    content_projector,
    final_projector,
    logit_multipliers,
    premixture_rescaler,
    specialist_switch_tensor,
    specialist_widen_tensor,
    specialist_shrink_tensor,
    picked_specialist_labels,
    specialist_shares,
):
    specialist_slot = lax.axis_index("exp")
    exp_count = lax.axis_size("exp")
    rows_all = lax.all_gather(residual_deposit_sequence, "exp", axis=0, tiled=True)
    rescaled_entries = norm_rows(rows_all, premix_rescaler).astype(jnp.bfloat16)
    local_lane_count = asking_projector.shape[1] // PER_LANE_DIM
    device_scratch = lax.dynamic_slice_in_dim(
        logit_multipliers, specialist_slot * local_lane_count, local_lane_count
    )
    partial_out = attend_hits(
        rescaled_entries,
        asking_projector,
        lookup_projector,
        content_projector,
        final_projector,
        device_scratch,
    )
    attention_full = lax.psum_scatter(
        partial_out.astype(jnp.bfloat16), "exp", scatter_dimension=0, tiled=True
    ).astype(jnp.float32)
    attention_update = attention_full.astype(jnp.bfloat16)
    residual = residual_deposit_sequence.astype(jnp.float32) + attention_full
    expert_in = norm_rows(residual, premixture_rescaler).astype(jnp.bfloat16)
    row_count = expert_in.shape[1]
    local_experts = specialist_switch_tensor.shape[0]
    expert_count = local_experts * exp_count
    own_ids = lax.dynamic_slice_in_dim(picked_specialist_labels, specialist_slot, 1, 0)
    own_gates = lax.dynamic_slice_in_dim(specialist_shares, specialist_slot, 1, 0).reshape(
        row_count * TOP
    )
    slot_of, tables = slot_tables(own_ids, expert_count)
    outgoing = jnp.take(expert_in[0], tables[0].reshape(expert_count * CAP), axis=0)
    outgoing = outgoing.reshape(exp_count, local_experts, CAP, D)
    produced = run_experts(
        lax.all_to_all(outgoing, "exp", split_axis=0, concat_axis=0, tiled=True),
        specialist_switch_tensor,
        specialist_widen_tensor,
        specialist_shrink_tensor,
    )
    returned = lax.all_to_all(produced, "exp", split_axis=0, concat_axis=0, tiled=True)
    position = own_ids.reshape(row_count * TOP) * CAP + slot_of[0]
    values = jnp.take(returned.reshape(expert_count * CAP, D), position, axis=0).astype(jnp.float32)
    combined = jnp.sum((values * own_gates[:, None]).reshape(row_count, TOP, D), axis=1)
    expert_update = combined.astype(jnp.bfloat16)[None]
    return (attention_update, expert_update)


def solution(mesh):
    placed = (
        P("exp", "blk", None),
        P(),
        P(None, "exp"),
        P(None, "exp"),
        P(None, "exp"),
        P("exp", None),
        P(),
        P(),
        P("exp", None, None),
        P("exp", None, None),
        P("exp", None, None),
        P(None, "blk", None),
        P(None, "blk", None),
    )
    return jax.shard_map(
        body,
        mesh=mesh,
        in_specs=placed,
        out_specs=(P("exp", "blk", None), P("exp", "blk", None)),
        check_vma=False,
    )
```

profile of v0, /device:TPU:0, one launch (start us, length us, event | category | flops | bytes accessed | tf_op | source)
XLA Modules:
  0.0 258.9 jit_solution(3094345826512784104)
XLA Ops:
  8.0 41.4 %all-gather.6.cloned.1.call-done = bf16[4,128,1536]{2,1,0:T(8,128)(2,1)} async-done(((bf16[1,128,1536]{2,1,0:T(8,128)(2,1)}), bf16[4,128,1536]{2,1,0:T(8,128)(2,1)}) %all-gather.6.cloned.1.call-update) | async-done | bytes 1572880 | tf_op jit(solution)/shard_map/all_gather | solution.py:128
  49.4 1.9 fusion.1
  51.4 1.5 multiply_reduce_fusion.3
  53.7 2.7 %convolution_convert_fusion.1 = bf16[4,128,128]{2,1,0:T(8,128)(2,1)} fusion(bf16[4,128,1536]{2,1,0:T(8,128)(2,1)} %all-gather.6.cloned.1.call-done, f32[1536]{0:T(1024)S(1)} %copy-done.9, f32[4,128]{1,0:T(4,128)S(1)} %add_rsqrt_fusion.3, bf16[1536,128]{1,0:T(8,128)(2,1)S(1)} %copy-done.8), kind=kOutput, calls=%fused_computation.35 | convolution fusion | flops 204537856 | bytes 2105344 | tf_op jit(solution)/shard_map/std,de->ste/dot_general | solution.py:48
  56.6 3.7 %fusion.70 = (f32[4,128,384]{2,1,0:T(8,128)S(1)}, f32[4,128,384]{2,1,0:T(8,128)}) fusion(bf16[1536,384]{1,0:T(8,128)(2,1)} %param.15, bf16[4,128,1536]{2,1,0:T(8,128)(2,1)} %all-gather.6.cloned.1.call-done, f32[1536]{0:T(1024)S(1)} %copy-done.9, f32[4,128]{1,0:T(4,128)S(1)} %add_rsqrt_fusion.3), kind=kOutput, calls=%fused_computation.101 | convolution fusion | flops 607322112 | bytes 4333568 | tf_op jit(solution)/shard_map/std,de->ste/dot_general | solution.py:36
  61.4 1.4 copy.52
  64.0 12.2 %all-gather.8.cloned.1.call-done = bf16[4,1024,128]{1,2,0:T(8,128)(2,1)} async-done(((bf16[4,128,128]{1,2,0:T(8,128)(2,1)}), bf16[4,1024,128]{1,2,0:T(8,128)(2,1)}) %all-gather.8.cloned.1.call-update) | async-done | bytes 1048592 | tf_op jit(solution)/shard_map/all_gather | solution.py:57
  76.2 5.4 %bitcast_reduce_fusion = (f32[4,3,128]{2,1,0:T(4,128)S(1)}, f32[4,1024,128,3]{2,1,3,0:T(8,128)}) fusion(f32[3]{0:T(128)S(1)} %dynamic-slice_multiply_fusion, f32[4,128,3,128]{1,3,2,0:T(8,128)S(1)} %bitcast.150, f32[4,128,3]{1,2,0:T(4,128)S(1)} %add_rsqrt_fusion.1, bf16[4,1024,128]{1,2,0:T(8,128)(2,1)} %all-gather.8.cloned.1.call-done), kind=kOutput, calls=%fused_computation.3 | convolution fusion | flops 406190592 | bytes 8138764 | tf_op jit(solution)/shard_map/sikgd,sjkd->skgij/dot_general | solution.py:59
  81.6 20.6 %all-gather.10.cloned.1.call-done = bf16[4,1024,128]{2,1,0:T(8,128)(2,1)} async-done(((bf16[4,128,128]{2,1,0:T(8,128)(2,1)}), bf16[4,1024,128]{2,1,0:T(8,128)(2,1)}) %all-gather.10.cloned.1.call-update) | async-done | bytes 1048592 | tf_op jit(solution)/shard_map/all_gather | solution.py:58
  102.2 4.4 %multiply_reduce_fusion.2 = (f32[4,3,128]{2,1,0:T(4,128)S(1)}, f32[4,3,128,128]{2,3,1,0:T(8,128)S(1)}) fusion(f32[4,3,128]{2,1,0:T(4,128)S(1)} %get-tuple-element.8, bf16[4,1024,128]{2,1,0:T(8,128)(2,1)} %all-gather.10.cloned.1.call-done, f32[4,1024,128,3]{2,1,3,0:T(8,128)} %get-tuple-element.9, f32[3]{0:T(128)S(1)} %dynamic-slice_multiply_fusion), kind=kOutput, calls=%fused_computation.50 | convolution fusion | flops 406387200 | bytes 8138764 | tf_op jit(solution)/shard_map/skgij,sjkd->skgid/dot_general | solution.py:64
  106.7 2.2 fusion.8
  111.1 11.2 %scatter_fusion = s32[8,64]{1,0:T(8,128)S(1)} fusion(s32[8,64]{1,0:T(8,128)S(1)} %broadcast.318, s32[256]{0:T(256)S(1)} %bitcast.148, s32[256]{0:T(256)S(1)} %bitcast.159), kind=kCustom, calls=%fused_computation.2 | custom fusion | bytes 5120 | tf_op jit(solution)/shard_map/scatter | solution.py:91
  122.4 22.0 %reduce-scatter.2.cloned.1.call-done = bf16[1,128,1536]{2,1,0:T(8,128)(2,1)} async-done(((bf16[4,128,1536]{2,1,0:T(8,128)(2,1)}), bf16[1,128,1536]{2,1,0:T(8,128)(2,1)}) %reduce-scatter.2.cloned.1.call-update) | async-done | bytes 393232 | tf_op jit(solution)/shard_map/reduce_scatter | solution.py:142
  144.3 1.2 multiply_reduce_fusion.1
  146.7 3.0 %gather_fusion = bf16[512,1536]{1,0:T(8,128)(2,1)} fusion(bf16[128,1536]{1,0:T(8,128)(2,1)S(1)} %fusion.60, s32[1024]{0:T(1024)S(1)} %pad_clamp_fusion.1), kind=kCustom, calls=%fused_computation | custom fusion | bytes 3147776 | tf_op jit(solution)/shard_map/jit(_take)/gather | solution.py:156
  149.7 1.6 broadcast_select_fusion
  151.3 39.7 %all_to_all.10 = bf16[4,2,64,1536]{3,2,1,0:T(8,128)(2,1)S(1)} all-to-all(bf16[4,2,64,1536]{3,2,1,0:T(8,128)(2,1)S(1)} %broadcast_select_fusion), channel_id=1, replica_groups=mesh['blk'=8,'exp'=4] {'exp'}, dimensions={0} | all-to-all | bytes 3145728 | tf_op jit(solution)/shard_map/all_to_all | solution.py:159
  193.2 5.1 %fusion.9 = bf16[4,2,64,1536]{3,2,0,1:T(8,128)(2,1)} fusion(bf16[2,384,1536]{2,1,0:T(8,128)(2,1)S(1)} %copy-done, bf16[2,1536,384]{2,1,0:T(8,128)(2,1)} %param.22, bf16[4,2,64,1536]{3,2,1,0:T(8,128)(2,1)} %copy-done.3, f32[4,2,64,384]{3,2,0,1:T(8,128)S(1)} %fusion.17), kind=kOutput, calls=%fused_computation.18 | convolution fusion | flops 1209925632 | bytes 8650752 | tf_op jit(solution)/shard_map/sjcf,jfd->sjcd/dot_general | solution.py:106
  198.3 2.7 %copy.65 = bf16[4,2,64,1536]{3,2,1,0:T(8,128)(2,1)} copy(bf16[4,2,64,1536]{3,2,0,1:T(8,128)(2,1)} %fusion.9) | data formatting | bytes 3145728 | tf_op jit(solution)/shard_map/convert_element_type | solution.py:108
  200.9 4.3 %all-to-all-start.1 = ((bf16[4,2,64,1536]{3,2,1,0:T(8,128)(2,1)}), bf16[4,2,64,1536]{3,2,1,0:T(8,128)(2,1)}, u32[]{:S(2)}, u32[]{:S(2)}) async-start(bf16[4,2,64,1536]{3,2,1,0:T(8,128)(2,1)} %copy.65), calls=%async_computation.2 | async-start | bytes 3145728 | tf_op jit(solution)/shard_map/all_to_all | solution.py:164
  206.7 35.1 %all-to-all-done.1 = bf16[4,2,64,1536]{3,2,1,0:T(8,128)(2,1)} async-done(((bf16[4,2,64,1536]{3,2,1,0:T(8,128)(2,1)}), bf16[4,2,64,1536]{3,2,1,0:T(8,128)(2,1)}, u32[]{:S(2)}, u32[]{:S(2)}) %all-to-all-start.1) | async-done | bytes 1572896 | tf_op jit(solution)/shard_map/all_to_all | solution.py:164
  241.8 4.5 %gather_fusion.1 = bf16[256,1536]{1,0:T(8,128)(2,1)} fusion(bf16[512,1536]{1,0:T(8,128)(2,1)} %bitcast.38, s32[1024]{0:T(1024)S(1)} %pad_clamp_fusion), kind=kCustom, calls=%fused_computation.1 | custom fusion | bytes 1573888 | tf_op jit(solution)/shard_map/jit(_take)/gather | solution.py:166
  246.3 2.2 gather.15
  248.4 3.9 %multiply_reduce_fusion = bf16[128,1536]{1,0:T(8,128)(2,1)} fusion(bf16[128,2,1536]{2,1,0:T(2,128)(2,1)S(1)} %gather.15, pred[128,2]{1,0:T(8,128)(4,1)S(1)} %copy.61, f32[128,2]{1,0:T(8,128)S(1)} %copy.67), kind=kLoop, calls=%fused_computation.24 | loop fusion | flops 1376256 | bytes 1180928 | tf_op jit(solution)/shard_map/reduce_sum | solution.py:167
  (71 shorter events, 11.0 us)
Async XLA Ops:
  7.2 186.0 %copy-start = (bf16[2,384,1536]{2,1,0:T(8,128)(2,1)S(1)}, bf16[2,384,1536]{2,1,0:T(8,128)(2,1)}, u32[]{:S(2)}) copy-start(bf16[2,384,1536]{2,1,0:T(8,128)(2,1)} %param.23) | copy-start | bytes 7077892
  7.2 44.2 %copy-start.7 = (bf16[1536,128]{1,0:T(8,128)(2,1)S(1)}, bf16[1536,128]{1,0:T(8,128)(2,1)}, u32[]{:S(2)}) copy-start(bf16[1536,128]{1,0:T(8,128)(2,1)} %param.16) | copy-start | bytes 1179652
  7.2 42.2 %all-gather.6.cloned.1.call-start = ((), (), s32[]{:S(2)}) async-start(), calls=%async_computation.3 | async-start | bytes 1966080 | tf_op jit(solution)/shard_map/all_gather | solution.py:128
  7.9 68.3 %all-gather.8.cloned.1.call-start = ((), (), s32[]{:S(2)}) async-start(), calls=%async_computation.5 | async-start | bytes 1179648 | tf_op jit(solution)/shard_map/all_gather | solution.py:57
  49.4 1.9 copy-start.2
  51.4 2.3 copy-start.8
  51.4 2.3 copy-start.9
  53.6 2.9 %copy-start.10 = (f32[12]{0:T(128)S(1)}, f32[12]{0:T(128)}, u32[]{:S(2)}) copy-start(f32[12]{0:T(128)} %param.19) | copy-start | bytes 148
  53.6 48.6 %all-gather.10.cloned.1.call-start = ((), (), s32[]{:S(2)}) async-start(), calls=%async_computation.6 | async-start | bytes 1179648 | tf_op jit(solution)/shard_map/all_gather | solution.py:58
  56.4 87.9 %reduce-scatter.2.cloned.1.call-start = ((), (), s32[]{:S(2)}) async-start(), calls=%async_computation.4 | async-start | bytes 1966080 | tf_op jit(solution)/shard_map/reduce_scatter | solution.py:142
  102.2 4.5 %copy-start.4 = (bf16[384,1536]{1,0:T(8,128)(2,1)S(1)}, bf16[384,1536]{1,0:T(8,128)(2,1)}, u32[]{:S(2)}) copy-start(bf16[384,1536]{1,0:T(8,128)(2,1)} %param.18) | copy-start | bytes 3538948
  108.9 35.4 %copy-start.1 = (bf16[1,128,1536]{2,1,0:T(8,128)(2,1)S(1)}, bf16[1,128,1536]{2,1,0:T(8,128)(2,1)}, u32[]{:S(2)}) copy-start(bf16[1,128,1536]{2,1,0:T(8,128)(2,1)} %param.13) | copy-start | bytes 1179652
  110.0 35.5 %copy-start.5 = (f32[1536]{0:T(1024)S(1)}, f32[1536]{0:T(1024)}, u32[]{:S(2)}) copy-start(f32[1536]{0:T(1024)} %param.20) | copy-start | bytes 18436
  151.3 40.8 %copy-start.6 = (bf16[2,1536,384]{2,1,0:T(8,128)(2,1)S(1)}, bf16[2,1536,384]{2,1,0:T(8,128)(2,1)}, u32[]{:S(2)}) copy-start(bf16[2,1536,384]{2,1,0:T(8,128)(2,1)} %param.21) | copy-start | bytes 7077892
  191.0 1.1 copy-start.3
  200.9 40.9 %all-to-all-start.1 = ((bf16[4,2,64,1536]{3,2,1,0:T(8,128)(2,1)}), bf16[4,2,64,1536]{3,2,1,0:T(8,128)(2,1)}, u32[]{:S(2)}, u32[]{:S(2)}) async-start(bf16[4,2,64,1536]{3,2,1,0:T(8,128)(2,1)} %copy.65), calls=%async_computation.2 | async-start | bytes 3145728 | tf_op jit(solution)/shard_map/all_to_all | solution.py:164
Sparse Core Ops, SparseCore 0:
  9.6 39.7 all-gather.5
  53.8 22.4 all-gather.7
  78.7 23.4 all-gather.9
  109.0 35.2 reduce-scatter.1
where the time goes:
time: 260 us; the launch traced here: 259 us
  waiting for transfers between devices  132 us (51%)
  blocking collectives  39.7 us (15%)
  local copies, waits for them, and re-layouts  29.3 us (11%)
  matrix products  26 us (10%)
  between operations  14.1 us (5%)
  other arithmetic  13.3 us (5%)
  starting transfers between devices  4.49 us (2%)
    all_gather x1, waiting for transfers between devices, body(): lax.all_gather(residual_deposit_sequence, 'exp', axis=0, tiled=True)  41.4 us
    all_to_all x1, blocking collectives, body(): lax.all_to_all(outgoing, 'exp', split_axis=0, concat_axis=0, tiled=True)  39.7 us
    all_to_all x1, waiting for transfers between devices, body(): lax.all_to_all(produced, 'exp', split_axis=0, concat_axis=0, tiled=True)  35.1 us
    reduce_scatter x1, waiting for transfers between devices, body(): lax.psum_scatter(partial_out.astype(jnp.bfloat16), 'exp', scatter_dimensi...  22 us
    all_gather x1, waiting for transfers between devices, attend_hits(): value_piece = lax.all_gather(value_heads, 'blk', axis=1, tiled=True)  20.6 us
    all_gather x1, waiting for transfers between devices, attend_hits(): key_piece = lax.all_gather(key_heads, 'blk', axis=1, tiled=True)  12.2 us
    scatter x1, local copies, waits for them, and re-layouts, slot_tables(): tables = jnp.zeros((events, expert_count, CAP), jnp.int32).at[event_index...  11.2 us
    gather x2, local copies, waits for them, and re-layouts, body(): jnp.take(returned.reshape(expert_count * CAP, D), position, axis=0)  6.65 us
  transfers between devices with their start and end apart: 5, of which 5 were waited for; matrix products, arithmetic and copies ran while one was open for 12% of the time, Pallas kernels for 0%

commit v1 on v0

--- a/solution.py
+++ b/solution.py
@@ -29,6 +29,42 @@
     final_projector,
     logit_multipliers,
 ):
+
+    def recover_state_up(net_axis, view):
+        n_now = lax.axis_size(net_axis)
+        odd = lax.axis_index(net_axis)
+        cards = []
+        inter, z, x_new = (n_now, odd, view.shape[1])
+        for at, k in enumerate(view.shape):
+            cards.append(k * inter if at == 1 else k)
+        local_next = finding = view
+        o_now = lax.dynamic_update_slice_in_dim(
+            jnp.zeros(cards, view.dtype), view, z * x_new, axis=1
+        )
+        k0 = 1
+        while k0 < inter // 2 + 1:
+            rack = []
+            at = 0
+            while at < inter:
+                rack.append((at, (at + 1) % inter))
+                at += 1
+            local_next = lax.ppermute(local_next, net_axis, rack)
+            o_now = lax.dynamic_update_slice_in_dim(
+                o_now, local_next, (z - k0) % inter * x_new, axis=1
+            )
+            if 2 * k0 < inter:
+                block_list = []
+                at = 0
+                while at < inter:
+                    block_list.append((at, (at - 1) % inter))
+                    at += 1
+                finding = lax.ppermute(finding, net_axis, block_list)
+                o_now = lax.dynamic_update_slice_in_dim(
+                    o_now, finding, (z + k0) % inter * x_new, axis=1
+                )
+            k0 = k0 + 1
+        return o_now
+
     events, row_count, model_width = rescaled_entries.shape
     common_key_heads = lookup_projector.shape[1] // PER_LANE_DIM
     local_lane_count = asking_projector.shape[1] // PER_LANE_DIM
@@ -55,7 +91,7 @@
         common_key_heads, askers_per_lookup
     )
     key_piece = lax.all_gather(key_heads, "blk", axis=1, tiled=True)
-    value_piece = lax.all_gather(value_heads, "blk", axis=1, tiled=True)
+    value_piece = recover_state_up("blk", value_heads)
     scores = jnp.einsum(
         "sikgd,sjkd->skgij", query_heads, key_piece, preferred_element_type=jnp.float32
     )

time: 260 us -> 242 us (0.931)
  waiting for transfers between devices: 132 us -> 104 us
  local copies, waits for them, and re-layouts: 29.3 us -> 40.2 us
  starting transfers between devices: 4.49 us -> 12.8 us
  matrix products: 26 us -> 18.4 us
    all_gather x1 -> x0, waiting for transfers between devices: 20.6 us -> none  [attend_hits(): value_piece = lax.all_gather(value_heads, 'blk', axis=1, tiled=True)]
    all_gather x1, waiting for transfers between devices: 12.2 us -> 0.01 us  [attend_hits(): key_piece = lax.all_gather(key_heads, 'blk', axis=1, tiled=True)]
    ppermute x0 -> x7, starting transfers between devices: none -> 8.37 us  [the longest x3 8.19 us: recover_state_up(): finding = lax.ppermute(finding, net_axis, block_list)]
    ppermute x0 -> x7, waiting for transfers between devices: none -> 5.29 us  [the longest x4 4.05 us: recover_state_up(): local_next = lax.ppermute(local_next, net_axis, rack)]
    dynamic_update_slice x0 -> x8, local copies, waits for them, and re-layouts: none -> 4.87 us  [the longest x4 2.75 us: recover_state_up(): lax.dynamic_update_slice_in_dim(o_now, local_next, (z - k0) % inter * x_n...]
    another operation x1 -> x9, local copies, waits for them, and re-layouts: 0.01 us -> 3.73 us
    dot_general x1, matrix products: 4.44 us -> 1.43 us  [attend_hits(): jnp.einsum('skgij,sjkd->skgid', expo.astype(jnp.bfloat16), value_piece, p...]
  transfers between devices with their start and end apart: 5 -> 11, of which waited for: 5 -> 7; matrix products, arithmetic and copies ran while one was open for 12% -> 13% of each run, Pallas kernels for 0% -> 0%
where the time goes in v1:
time: 242 us
  waiting for transfers between devices  104 us (43%)
  local copies, waits for them, and re-layouts  40.2 us (17%)
  blocking collectives  39.7 us (16%)
  matrix products  18.4 us (8%)
  between operations  14.3 us (6%)
  starting transfers between devices  12.8 us (5%)
  other arithmetic  12.2 us (5%)
    all_gather x1, waiting for transfers between devices, body(): lax.all_gather(residual_deposit_sequence, 'exp', axis=0, tiled=True)  41.3 us
    all_to_all x1, blocking collectives, body(): lax.all_to_all(outgoing, 'exp', split_axis=0, concat_axis=0, tiled=True)  39.7 us
    all_to_all x1, waiting for transfers between devices, body(): lax.all_to_all(produced, 'exp', split_axis=0, concat_axis=0, tiled=True)  35.4 us
    reduce_scatter x1, waiting for transfers between devices, body(): lax.psum_scatter(partial_out.astype(jnp.bfloat16), 'exp', scatter_dimensi...  21.4 us
    scatter x1, local copies, waits for them, and re-layouts, slot_tables(): tables = jnp.zeros((events, expert_count, CAP), jnp.int32).at[event_index...  11.2 us
    ppermute x3, starting transfers between devices, recover_state_up(): finding = lax.ppermute(finding, net_axis, block_list)  8.19 us
    gather x2, local copies, waits for them, and re-layouts, body(): jnp.take(returned.reshape(expert_count * CAP, D), position, axis=0)  6.66 us
    dot_general x1, matrix products, run_experts(): jnp.einsum('sjcf,jfd->sjcd', hidden, specialist_shrink_tensor, preferred_...  5.11 us
  transfers between devices with their start and end apart: 11, of which 7 were waited for; matrix products, arithmetic and copies ran while one was open for 13% of the time, Pallas kernels for 0%

profile of v1, /device:TPU:0, one launch (start us, length us, event | category | flops | bytes accessed | tf_op | source)
XLA Modules:
  0.0 241.7 jit_solution(1904841760679170357)
XLA Ops:
  8.1 41.3 %all-gather.4.cloned.1.call-done = bf16[4,128,1536]{2,1,0:T(8,128)(2,1)} async-done(((bf16[1,128,1536]{2,1,0:T(8,128)(2,1)}), bf16[4,128,1536]{2,1,0:T(8,128)(2,1)}) %all-gather.4.cloned.1.call-update) | async-done | bytes 1572880 | tf_op jit(solution)/shard_map/all_gather | solution.py:164
  49.4 1.9 fusion.1
  53.1 2.8 %convolution_convert_fusion.1 = bf16[4,128,128]{2,1,0:T(8,128)(2,1)} fusion(bf16[4,128,1536]{2,1,0:T(8,128)(2,1)} %all-gather.4.cloned.1.call-done, f32[1536]{0:T(1024)S(1)} %copy-done.13, f32[4,128]{1,0:T(4,128)S(1)} %add_rsqrt_fusion.3, bf16[1536,128]{1,0:T(8,128)(2,1)S(1)} %copy-done.12), kind=kOutput, calls=%fused_computation.35 | convolution fusion | flops 204537856 | bytes 2105344 | tf_op jit(solution)/shard_map/std,de->ste/dot_general | solution.py:84
  55.9 2.6 %collective-permute-start.1 = (bf16[4,128,1,128]{3,1,0,2:T(8,128)(2,1)}, bf16[4,128,1,128]{3,1,0,2:T(8,128)(2,1)S(1)}, u32[]{:S(2)}, u32[]{:S(2)}) collective-permute-start(bf16[4,128,1,128]{3,1,0,2:T(8,128)(2,1)} %bitcast.9), channel_id=1, source_target_pairs={{0,28},{4,0},{8,4},{12,8},{16,12},{20,16},{24,20},{28,24},{1,29},{... | collective-permute-start | bytes 393224 | tf_op jit(solution)/shard_map/ppermute | solution.py:61
  58.5 2.2 fusion.71
  64.5 1.4 copy.75
  66.9 2.7 %collective-permute-start.3 = (bf16[4,128,1,128]{3,1,0,2:T(8,128)(2,1)S(1)}, bf16[4,128,1,128]{3,1,0,2:T(8,128)(2,1)}, u32[]{:S(2)}, u32[]{:S(2)}) collective-permute-start(bf16[4,128,1,128]{3,1,0,2:T(8,128)(2,1)S(1)} %collective-permute-done.1), channel_id=1, source_target_pairs={{0,28},{4,0},{8,4},{12,8},{16,12},{20,16},{24,20},{28,24},{1,29},{... | collective-permute-start | bytes 393224 | tf_op jit(solution)/shard_map/ppermute | solution.py:61
  74.3 2.9 %collective-permute-start.5 = (bf16[4,128,1,128]{3,1,0,2:T(8,128)(2,1)}, bf16[4,128,1,128]{3,1,0,2:T(8,128)(2,1)S(1)}, u32[]{:S(2)}, u32[]{:S(2)}) collective-permute-start(bf16[4,128,1,128]{3,1,0,2:T(8,128)(2,1)} %collective-permute-done.3), channel_id=1, source_target_pairs={{0,28},{4,0},{8,4},{12,8},{16,12},{20,16},{24,20},{28,24},{1,29},{... | collective-permute-start | bytes 393224 | tf_op jit(solution)/shard_map/ppermute | solution.py:61
  81.0 2.6 %collective-permute-done.6 = bf16[4,128,1,128]{3,1,0,2:T(8,128)(2,1)} collective-permute-done((bf16[4,128,1,128]{3,1,0,2:T(8,128)(2,1)S(1)}, bf16[4,128,1,128]{3,1,0,2:T(8,128)(2,1)}, u32[]{:S(2)}, u32[]{:S(2)}) %collective-permute-start.6) | collective-permute-done | bytes 131104 | tf_op jit(solution)/shard_map/ppermute | solution.py:51
  85.4 2.9 %bitcast_reduce_fusion = (f32[4,3,128]{2,1,0:T(4,128)S(1)}, f32[4,1024,128,3]{2,1,3,0:T(8,128)S(1)}) fusion(f32[3]{0:T(128)S(1)} %dynamic-slice_multiply_fusion, f32[4,128,3,128]{1,3,2,0:T(8,128)S(1)} %bitcast.157, f32[4,128,3]{1,2,0:T(4,128)S(1)} %add_rsqrt_fusion.1, bf16[4,1024,128]{1,2,0:T(8,128)(2,1)} %all-gather.6.cloned.1.call-done), kind=kOutput, calls=%fused_computation.3 | convolution fusion | flops 406190592 | bytes 8138764 | tf_op jit(solution)/shard_map/sikgd,sjkd->skgij/dot_general | solution.py:95
  88.3 1.4 multiply_reduce_fusion.2
  89.8 2.2 fusion.8
  94.4 11.2 %scatter_fusion = s32[8,64]{1,0:T(8,128)S(1)} fusion(s32[8,64]{1,0:T(8,128)S(1)} %broadcast.333, s32[256]{0:T(256)S(1)} %bitcast.155, s32[256]{0:T(256)S(1)} %bitcast.170), kind=kCustom, calls=%fused_computation.2 | custom fusion | bytes 5120 | tf_op jit(solution)/shard_map/scatter | solution.py:127
  105.7 21.4 %reduce-scatter.2.cloned.1.call-done = bf16[1,128,1536]{2,1,0:T(8,128)(2,1)} async-done(((bf16[4,128,1536]{2,1,0:T(8,128)(2,1)}), bf16[1,128,1536]{2,1,0:T(8,128)(2,1)}) %reduce-scatter.2.cloned.1.call-update) | async-done | bytes 393232 | tf_op jit(solution)/shard_map/reduce_scatter | solution.py:178
  129.5 2.9 %gather_fusion = bf16[512,1536]{1,0:T(8,128)(2,1)} fusion(bf16[128,1536]{1,0:T(8,128)(2,1)S(1)} %fusion.60, s32[1024]{0:T(1024)S(1)} %pad_clamp_fusion.1), kind=kCustom, calls=%fused_computation | custom fusion | bytes 3147776 | tf_op jit(solution)/shard_map/jit(_take)/gather | solution.py:192
  132.5 1.6 broadcast_select_fusion
  134.1 39.7 %all_to_all.10 = bf16[4,2,64,1536]{3,2,1,0:T(8,128)(2,1)S(1)} all-to-all(bf16[4,2,64,1536]{3,2,1,0:T(8,128)(2,1)S(1)} %broadcast_select_fusion), channel_id=1, replica_groups=mesh['blk'=8,'exp'=4] {'exp'}, dimensions={0} | all-to-all | bytes 3145728 | tf_op jit(solution)/shard_map/all_to_all | solution.py:195
  176.0 5.1 %fusion.9 = bf16[4,2,64,1536]{3,2,0,1:T(8,128)(2,1)} fusion(bf16[2,384,1536]{2,1,0:T(8,128)(2,1)S(1)} %copy-done, bf16[2,1536,384]{2,1,0:T(8,128)(2,1)} %param.22, bf16[4,2,64,1536]{3,2,1,0:T(8,128)(2,1)} %copy-done.4, f32[4,2,64,384]{3,2,0,1:T(8,128)S(1)} %fusion.17), kind=kOutput, calls=%fused_computation.18 | convolution fusion | flops 1209925632 | bytes 8650752 | tf_op jit(solution)/shard_map/sjcf,jfd->sjcd/dot_general | solution.py:142
  181.1 2.7 %copy.95 = bf16[4,2,64,1536]{3,2,1,0:T(8,128)(2,1)} copy(bf16[4,2,64,1536]{3,2,0,1:T(8,128)(2,1)} %fusion.9) | data formatting | bytes 3145728 | tf_op jit(solution)/shard_map/convert_element_type | solution.py:144
  183.7 4.3 %all-to-all-start.1 = ((bf16[4,2,64,1536]{3,2,1,0:T(8,128)(2,1)}), bf16[4,2,64,1536]{3,2,1,0:T(8,128)(2,1)}, u32[]{:S(2)}, u32[]{:S(2)}) async-start(bf16[4,2,64,1536]{3,2,1,0:T(8,128)(2,1)} %copy.95), calls=%async_computation.2 | async-start | bytes 3145728 | tf_op jit(solution)/shard_map/all_to_all | solution.py:200
  189.3 35.4 %all-to-all-done.1 = bf16[4,2,64,1536]{3,2,1,0:T(8,128)(2,1)} async-done(((bf16[4,2,64,1536]{3,2,1,0:T(8,128)(2,1)}), bf16[4,2,64,1536]{3,2,1,0:T(8,128)(2,1)}, u32[]{:S(2)}, u32[]{:S(2)}) %all-to-all-start.1) | async-done | bytes 1572896 | tf_op jit(solution)/shard_map/all_to_all | solution.py:200
  224.6 4.5 %gather_fusion.1 = bf16[256,1536]{1,0:T(8,128)(2,1)} fusion(bf16[512,1536]{1,0:T(8,128)(2,1)} %bitcast.47, s32[1024]{0:T(1024)S(1)} %pad_clamp_fusion), kind=kCustom, calls=%fused_computation.1 | custom fusion | bytes 1573888 | tf_op jit(solution)/shard_map/jit(_take)/gather | solution.py:202
  229.1 2.2 gather.15
  231.3 3.9 %multiply_reduce_fusion = bf16[128,1536]{1,0:T(8,128)(2,1)} fusion(bf16[128,2,1536]{2,1,0:T(2,128)(2,1)S(1)} %gather.15, pred[128,2]{1,0:T(8,128)(4,1)S(1)} %copy.91, f32[128,2]{1,0:T(8,128)S(1)} %copy.97), kind=kLoop, calls=%fused_computation.24 | loop fusion | flops 1376256 | bytes 1180928 | tf_op jit(solution)/shard_map/reduce_sum | solution.py:203
  (107 shorter events, 25.6 us)
Async XLA Ops:
  7.2 168.8 %copy-start = (bf16[2,384,1536]{2,1,0:T(8,128)(2,1)S(1)}, bf16[2,384,1536]{2,1,0:T(8,128)(2,1)}, u32[]{:S(2)}) copy-start(bf16[2,384,1536]{2,1,0:T(8,128)(2,1)} %param.23) | copy-start | bytes 7077892
  7.2 44.2 %copy-start.13 = (f32[1536]{0:T(1024)S(1)}, f32[1536]{0:T(1024)}, u32[]{:S(2)}) copy-start(f32[1536]{0:T(1024)} %param.14) | copy-start | bytes 18436
  7.2 44.2 %copy-start.11 = (bf16[1536,128]{1,0:T(8,128)(2,1)S(1)}, bf16[1536,128]{1,0:T(8,128)(2,1)}, u32[]{:S(2)}) copy-start(bf16[1536,128]{1,0:T(8,128)(2,1)} %param.16) | copy-start | bytes 1179652
  7.2 42.2 %all-gather.4.cloned.1.call-start = ((), (), s32[]{:S(2)}) async-start(), calls=%async_computation.3 | async-start | bytes 1966080 | tf_op jit(solution)/shard_map/all_gather | solution.py:164
  7.9 77.4 %all-gather.6.cloned.1.call-start = ((), (), s32[]{:S(2)}) async-start(), calls=%async_computation.5 | async-start | bytes 1179648 | tf_op jit(solution)/shard_map/all_gather | solution.py:93
  49.4 1.9 copy-start.2
  51.4 1.6 copy-start.14
  51.4 1.7 copy-start.12
  52.9 74.3 %reduce-scatter.2.cloned.1.call-start = ((), (), s32[]{:S(2)}) async-start(), calls=%async_computation.4 | async-start | bytes 1966080 | tf_op jit(solution)/shard_map/reduce_scatter | solution.py:178
  53.0 5.5 %copy-start.3 = (bf16[4,128,1536]{2,1,0:T(8,128)(2,1)S(1)}, bf16[4,128,1536]{2,1,0:T(8,128)(2,1)}, u32[]{:S(2)}) copy-start(bf16[4,128,1536]{2,1,0:T(8,128)(2,1)} %all-gather.4.cloned.1.call-done) | copy-start | bytes 4718596
  53.1 5.5 %copy-start.10 = (bf16[1536,384]{1,0:T(8,128)(2,1)S(1)}, bf16[1536,384]{1,0:T(8,128)(2,1)}, u32[]{:S(2)}) copy-start(bf16[1536,384]{1,0:T(8,128)(2,1)} %param.15) | copy-start | bytes 3538948
  55.9 10.0 %collective-permute-start = (bf16[4,128,1,128]{3,1,0,2:T(8,128)(2,1)}, bf16[4,128,1,128]{3,1,0,2:T(8,128)(2,1)S(1)}, u32[]{:S(2)}, u32[]{:S(2)}) collective-permute-start(bf16[4,128,1,128]{3,1,0,2:T(8,128)(2,1)} %bitcast.9), channel_id=1, source_target_pairs={{0,4},{4,8},{8,12},{12,16},{16,20},{20,24},{24,28},{28,0},{1,5},{5... | collective-permute-start | bytes 393224 | tf_op jit(solution)/shard_map/ppermute | solution.py:51
  55.9 10.9 %collective-permute-start.1 = (bf16[4,128,1,128]{3,1,0,2:T(8,128)(2,1)}, bf16[4,128,1,128]{3,1,0,2:T(8,128)(2,1)S(1)}, u32[]{:S(2)}, u32[]{:S(2)}) collective-permute-start(bf16[4,128,1,128]{3,1,0,2:T(8,128)(2,1)} %bitcast.9), channel_id=1, source_target_pairs={{0,28},{4,0},{8,4},{12,8},{16,12},{20,16},{24,20},{28,24},{1,29},{... | collective-permute-start | bytes 393224 | tf_op jit(solution)/shard_map/ppermute | solution.py:61
  66.0 5.5 %collective-permute-start.2 = (bf16[4,128,1,128]{3,1,0,2:T(8,128)(2,1)S(1)}, bf16[4,128,1,128]{3,1,0,2:T(8,128)(2,1)}, u32[]{:S(2)}, u32[]{:S(2)}) collective-permute-start(bf16[4,128,1,128]{3,1,0,2:T(8,128)(2,1)S(1)} %collective-permute-done), channel_id=1, source_target_pairs={{0,4},{4,8},{8,12},{12,16},{16,20},{20,24},{24,28},{28,0},{1,5},{5... | collective-permute-start | bytes 393224 | tf_op jit(solution)/shard_map/ppermute | solution.py:51
  66.9 6.4 %collective-permute-start.3 = (bf16[4,128,1,128]{3,1,0,2:T(8,128)(2,1)S(1)}, bf16[4,128,1,128]{3,1,0,2:T(8,128)(2,1)}, u32[]{:S(2)}, u32[]{:S(2)}) collective-permute-start(bf16[4,128,1,128]{3,1,0,2:T(8,128)(2,1)S(1)} %collective-permute-done.1), channel_id=1, source_target_pairs={{0,28},{4,0},{8,4},{12,8},{16,12},{20,16},{24,20},{28,24},{1,29},{... | collective-permute-start | bytes 393224 | tf_op jit(solution)/shard_map/ppermute | solution.py:61
  72.5 5.6 %collective-permute-start.4 = (bf16[4,128,1,128]{3,1,0,2:T(8,128)(2,1)}, bf16[4,128,1,128]{3,1,0,2:T(8,128)(2,1)S(1)}, u32[]{:S(2)}, u32[]{:S(2)}) collective-permute-start(bf16[4,128,1,128]{3,1,0,2:T(8,128)(2,1)} %collective-permute-done.2), channel_id=1, source_target_pairs={{0,4},{4,8},{8,12},{12,16},{16,20},{20,24},{24,28},{28,0},{1,5},{5... | collective-permute-start | bytes 393224 | tf_op jit(solution)/shard_map/ppermute | solution.py:51
  74.3 5.9 %collective-permute-start.5 = (bf16[4,128,1,128]{3,1,0,2:T(8,128)(2,1)}, bf16[4,128,1,128]{3,1,0,2:T(8,128)(2,1)S(1)}, u32[]{:S(2)}, u32[]{:S(2)}) collective-permute-start(bf16[4,128,1,128]{3,1,0,2:T(8,128)(2,1)} %collective-permute-done.3), channel_id=1, source_target_pairs={{0,28},{4,0},{8,4},{12,8},{16,12},{20,16},{24,20},{28,24},{1,29},{... | collective-permute-start | bytes 393224 | tf_op jit(solution)/shard_map/ppermute | solution.py:61
  78.2 5.4 %collective-permute-start.6 = (bf16[4,128,1,128]{3,1,0,2:T(8,128)(2,1)S(1)}, bf16[4,128,1,128]{3,1,0,2:T(8,128)(2,1)}, u32[]{:S(2)}, u32[]{:S(2)}) collective-permute-start(bf16[4,128,1,128]{3,1,0,2:T(8,128)(2,1)S(1)} %collective-permute-done.4), channel_id=1, source_target_pairs={{0,4},{4,8},{8,12},{12,16},{16,20},{20,24},{24,28},{28,0},{1,5},{5... | collective-permute-start | bytes 393224 | tf_op jit(solution)/shard_map/ppermute | solution.py:51
  85.4 2.9 %copy-start.7 = (bf16[4,1024,128]{1,2,0:T(8,128)(2,1)S(1)}, bf16[4,1024,128]{1,2,0:T(8,128)(2,1)}, u32[]{:S(2)}) copy-start(bf16[4,1024,128]{1,2,0:T(8,128)(2,1)} %constant_dynamic-update-slice_fusion) | copy-start | bytes 3145732
  88.3 1.5 copy-start.5
  92.0 35.2 %copy-start.1 = (bf16[1,128,1536]{2,1,0:T(8,128)(2,1)S(1)}, bf16[1,128,1536]{2,1,0:T(8,128)(2,1)}, u32[]{:S(2)}) copy-start(bf16[1,128,1536]{2,1,0:T(8,128)(2,1)} %param.13) | copy-start | bytes 1179652
  94.1 34.3 %copy-start.8 = (f32[1536]{0:T(1024)S(1)}, f32[1536]{0:T(1024)}, u32[]{:S(2)}) copy-start(f32[1536]{0:T(1024)} %param.20) | copy-start | bytes 18436
  134.1 40.8 %copy-start.9 = (bf16[2,1536,384]{2,1,0:T(8,128)(2,1)S(1)}, bf16[2,1536,384]{2,1,0:T(8,128)(2,1)}, u32[]{:S(2)}) copy-start(bf16[2,1536,384]{2,1,0:T(8,128)(2,1)} %param.21) | copy-start | bytes 7077892
  183.7 40.9 %all-to-all-start.1 = ((bf16[4,2,64,1536]{3,2,1,0:T(8,128)(2,1)}), bf16[4,2,64,1536]{3,2,1,0:T(8,128)(2,1)}, u32[]{:S(2)}, u32[]{:S(2)}) async-start(bf16[4,2,64,1536]{3,2,1,0:T(8,128)(2,1)} %copy.95), calls=%async_computation.2 | async-start | bytes 3145728 | tf_op jit(solution)/shard_map/all_to_all | solution.py:200
  (2 other events, 2.2 us)
Sparse Core Ops, SparseCore 0:
  9.6 39.7 all-gather.3
  53.0 24.0 all-gather.5
  92.1 35.0 reduce-scatter.1
